TPU v7x, 128 devices: a whole 4x4x4 slice. The times are simulated.
128 devices in a mesh: head: 8 (over x, core), ctx: 16 (over z, y).
Axes of the slice: x: 4, y: 4, z: 4, core: 2. Of those that a mesh axis runs over, the one named last changes fastest.
Arguments:
- queries: bfloat16 [128, 256, 4096], P('ctx', 'head'), may hold values from -6 to 6
- keys: bfloat16 [128, 256, 4096], P('ctx', 'head'), may hold values from -6 to 6
- values: bfloat16 [128, 256, 4096], P('ctx', 'head'), may hold values from -6 to 6
- grad_out: bfloat16 [128, 256, 4096], P('ctx', 'head'), may hold values from -24 to 24
- attn_out: bfloat16 [128, 256, 4096], P('ctx', 'head'), may hold values from -6 to 6
- lse: float32 [128, 32, 256], P('ctx', 'head'), may hold values from 5.5 to 7.5
- selected: int32 [128, 2], P('ctx'), may hold values from 0 to 119, as said below
- doc_lengths: int32 [4], replicated, may hold values from 1 to 32640, 32768 in all
Outputs:
- grad_q: bfloat16 [128, 256, 4096], P('ctx', None, 'head')
- grad_k: bfloat16 [128, 256, 4096], P('ctx', None, 'head')
- grad_v: bfloat16 [128, 256, 4096], P('ctx', None, 'head')
Inputs may be any that keep to these rules, and one draw needn't show every extreme that they name: `selected`: for query block i either both entries equal i (it selects nothing) or they are two different blocks j with the same o = j // 8, and o < i // 8. Among the 8 query blocks with one value of i // 8, at most 1 select blocks of any one o, and 1 is reached. For every value of i // 8 from 1 on, some query block selects blocks with o = 0.
All inputs are finite; a program needn't handle non-finite values.
Results may differ from a plain program's by a relative error of at most 0.0055.
Values may be sent and summed in bfloat16 or wider, within the bound.
A program may use at most 192 MiB of HBM per device.

v0:
```python
import jax
import jax.numpy as jnp
from jax import lax
from jax.sharding import PartitionSpec as P


def doc_of(positions, doc_lengths):
    ends = jnp.cumsum(doc_lengths)
    return jnp.sum((positions[..., None] >= ends).astype(jnp.int32), axis=-1)


def block_grads(query, grad_rows, key_rows, value_rows, lse_rows, delta_rows, allowed_rows, scale):
    scores = (
        jnp.einsum("grhd,gkhd->ghrk", query, key_rows, preferred_element_type=jnp.float32) * scale
    )
    probs = jnp.where(allowed_rows[:, None], jnp.exp(scores - lse_rows[..., None]), 0.0)
    prob_low = probs.astype(jnp.bfloat16)
    dprobs = jnp.einsum(
        "grhd,gkhd->ghrk", grad_rows, value_rows, preferred_element_type=jnp.float32
    )
    dscores = (probs * (dprobs - delta_rows[..., None])).astype(jnp.bfloat16)
    grad_query = (
        jnp.einsum("ghrk,gkhd->grhd", dscores, key_rows, preferred_element_type=jnp.float32) * scale
    )
    part_key = (
        jnp.einsum("ghrk,grhd->gkhd", dscores, query, preferred_element_type=jnp.float32) * scale
    )
    part_value = jnp.einsum(
        "ghrk,grhd->gkhd", prob_low, grad_rows, preferred_element_type=jnp.float32
    )
    return (grad_query, part_key, part_value)


def by_pairs(func, arrays):
    paired = tuple((array.reshape((array.shape[0] // 2, 2) + array.shape[1:]) for array in arrays))
    outcome = lax.map(lambda member: func(*member), paired)
    return tuple((result.reshape((result.shape[0] * 2,) + result.shape[2:]) for result in outcome))


def body(queries, keys, values, grad_out, attn_out, lse, selected, doc_lengths):
    blocks, rows_here, columns = queries.shape
    heads_here = lse.shape[1]
    head_count = lax.axis_size("head")
    ctx_count = lax.axis_size("ctx")
    width = columns // (heads_here * head_count)
    block_rows = rows_here * head_count
    columns_here = heads_here * width
    scale = width ** (-0.5)
    capacity = (blocks + ctx_count - 2) // (ctx_count - 1)
    here = lax.axis_index("ctx")
    split_shape = (blocks, block_rows, heads_here, width)
    delta_tokens = jnp.einsum(
        "brhd,brhd->brh",
        grad_out.reshape(blocks, rows_here, -1, width),
        attn_out.reshape(blocks, rows_here, -1, width),
        preferred_element_type=jnp.float32,
    )
    query_heads, key_heads, value_heads, grad_heads = (
        lax.all_to_all(queries, "head", split_axis=2, concat_axis=1, tiled=True),
        lax.all_to_all(keys, "head", split_axis=2, concat_axis=1, tiled=True),
        lax.all_to_all(values, "head", split_axis=2, concat_axis=1, tiled=True),
        lax.all_to_all(grad_out, "head", split_axis=2, concat_axis=1, tiled=True),
    )
    delta_heads = lax.all_to_all(delta_tokens, "head", split_axis=2, concat_axis=1, tiled=True)
    delta_heads = jnp.transpose(delta_heads, (0, 2, 1))
    local = jnp.arange(blocks, dtype=jnp.int32)
    rows = jnp.arange(block_rows, dtype=jnp.int32)
    own_ids = here * blocks + local
    own_docs = doc_of(own_ids[:, None] * block_rows + rows[None, :], doc_lengths)
    used = selected[:, 0] != own_ids
    owner = selected[:, 0] // blocks
    earlier = local[None, :] < local[:, None]
    sharing = (owner[None, :] == owner[:, None]) & used[None, :]
    rank = jnp.sum((earlier & sharing).astype(jnp.int32), axis=1)
    slot = jnp.where(used, owner * capacity + rank, ctx_count * capacity)
    causal = rows[:, None] >= rows[None, :]
    slots = ctx_count * 2 * capacity
    item_slot = (2 * slot[:, None] + jnp.arange(2, dtype=jnp.int32)[None, :]).reshape(-1)
    hits = item_slot[:, None] == jnp.arange(slots, dtype=jnp.int32)[None, :]
    wanted = jnp.sum(jnp.where(hits, (selected % blocks).reshape(-1)[:, None] + 1, 0), axis=0) - 1
    asked = lax.all_to_all(
        wanted.reshape(ctx_count, 2 * capacity), "ctx", split_axis=0, concat_axis=0, tiled=True
    ).reshape(-1)
    chosen = jnp.maximum(asked, 0)
    send_keys = jnp.take(key_heads, chosen, axis=0).reshape(
        ctx_count, 2 * capacity, block_rows, columns_here
    )
    send_values = jnp.take(value_heads, chosen, axis=0).reshape(
        ctx_count, 2 * capacity, block_rows, columns_here
    )
    got_keys, got_values = (
        lax.all_to_all(send_keys, "ctx", split_axis=0, concat_axis=0, tiled=True),
        lax.all_to_all(send_values, "ctx", split_axis=0, concat_axis=0, tiled=True),
    )
    place = jnp.minimum(item_slot, slots - 1)
    far_keys = jnp.take(got_keys.reshape(slots, block_rows, columns_here), place, axis=0).reshape(
        blocks, 2, block_rows, columns_here
    )
    far_values = jnp.take(
        got_values.reshape(slots, block_rows, columns_here), place, axis=0
    ).reshape(blocks, 2, block_rows, columns_here)
    all_keys = jnp.concatenate([key_heads[:, None], far_keys], axis=1).reshape(
        blocks, 3 * block_rows, heads_here, width
    )
    all_values = jnp.concatenate([value_heads[:, None], far_values], axis=1).reshape(
        blocks, 3 * block_rows, heads_here, width
    )
    far_docs = doc_of(selected[:, :, None] * block_rows + rows[None, None, :], doc_lengths).reshape(
        blocks, 2 * block_rows
    )
    key_docs = jnp.concatenate([own_docs, far_docs], axis=1)
    reach = jnp.concatenate([causal, jnp.ones((block_rows, 2 * block_rows), dtype=bool)], axis=1)
    open_far = jnp.concatenate(
        [
            jnp.ones((blocks, block_rows), dtype=bool),
            jnp.repeat(used[:, None], 2 * block_rows, axis=1),
        ],
        axis=1,
    )
    allowed = (own_docs[:, :, None] == key_docs[:, None, :]) & reach[None] & open_far[:, None, :]

    def pair_grads(query, grad_rows, key_rows, value_rows, lse_rows, delta_rows, allowed_rows):
        return block_grads(
            query, grad_rows, key_rows, value_rows, lse_rows, delta_rows, allowed_rows, scale
        )

    grad_query, part_key, part_value = by_pairs(
        pair_grads,
        (
            query_heads.reshape(split_shape),
            grad_heads.reshape(split_shape),
            all_keys,
            all_values,
            lse,
            delta_heads,
            allowed,
        ),
    )
    own_key = part_key[:, :block_rows].reshape(blocks, block_rows, columns_here)
    own_value = part_value[:, :block_rows].reshape(blocks, block_rows, columns_here)
    far_part_keys = (
        part_key[:, block_rows:].reshape(2 * blocks, block_rows, columns_here).astype(jnp.bfloat16)
    )
    far_part_values = (
        part_value[:, block_rows:]
        .reshape(2 * blocks, block_rows, columns_here)
        .astype(jnp.bfloat16)
    )
    source = jnp.sum(jnp.where(hits, jnp.arange(2 * blocks, dtype=jnp.int32)[:, None], 0), axis=0)
    back_keys = jnp.take(far_part_keys, source, axis=0).reshape(
        ctx_count, 2 * capacity, block_rows, columns_here
    )
    back_values = jnp.take(far_part_values, source, axis=0).reshape(
        ctx_count, 2 * capacity, block_rows, columns_here
    )
    come_keys, come_values = (
        lax.all_to_all(back_keys, "ctx", split_axis=0, concat_axis=0, tiled=True),
        lax.all_to_all(back_values, "ctx", split_axis=0, concat_axis=0, tiled=True),
    )
    pick = (asked[:, None] == local[None, :]).astype(jnp.bfloat16)
    add_keys = jnp.einsum(
        "sq,src->qrc",
        pick,
        come_keys.reshape(slots, block_rows, columns_here),
        preferred_element_type=jnp.float32,
    )
    add_values = jnp.einsum(
        "sq,src->qrc",
        pick,
        come_values.reshape(slots, block_rows, columns_here),
        preferred_element_type=jnp.float32,
    )
    grad_q = grad_query.reshape(blocks, block_rows, columns_here).astype(jnp.bfloat16)
    grad_k = (own_key + add_keys).astype(jnp.bfloat16)
    grad_v = (own_value + add_values).astype(jnp.bfloat16)
    return (grad_q, grad_k, grad_v)


def solution(mesh):
    in_specs = (
        P("ctx", "head", None),
        P("ctx", "head", None),
        P("ctx", "head", None),
        P("ctx", "head", None),
        P("ctx", "head", None),
        P("ctx", "head", None),
        P("ctx", None),
        P(),
    )
    out_specs = (P("ctx", None, "head"), P("ctx", None, "head"), P("ctx", None, "head"))
    return jax.shard_map(body, mesh=mesh, in_specs=in_specs, out_specs=out_specs, check_vma=False)
```

profile of v0, /device:TPU:0, one launch (start us, length us, event | category | flops | bytes accessed | tf_op | source)
XLA Modules:
  0.0 901.5 jit_solution(15278874825041744504)
XLA Ops:
  5.5 8.1 all-to-all-start.1
  25.5 9.2 %copy.155 = bf16[8,32,4096]{1,0,2:T(8,128)(2,1)} copy(bf16[8,32,4096]{2,1,0:T(8,128)(2,1)} %param.17) | data formatting | bytes 4194304 | tf_op args[1]
  34.7 11.2 %reshape.357 = bf16[8,2,65536]{2,1,0:T(2,128)(2,1)} reshape(bf16[4096,8,32]{2,1,0:T(8,128)(2,1)} %bitcast.205) | data formatting | bytes 4194304
  50.7 9.2 %copy.167 = bf16[8,32,4096]{1,0,2:T(8,128)(2,1)} copy(bf16[8,32,4096]{2,1,0:T(8,128)(2,1)} %param.18) | data formatting | bytes 4194304 | tf_op args[2]
  59.9 11.2 %reshape.363 = bf16[8,2,65536]{2,1,0:T(2,128)(2,1)} reshape(bf16[4096,8,32]{2,1,0:T(8,128)(2,1)} %bitcast.206) | data formatting | bytes 4194304
  71.1 6.9 all-to-all-done
  82.3 9.2 %copy.163 = bf16[8,32,4096]{1,0,2:T(8,128)(2,1)} copy(bf16[8,32,4096]{2,1,0:T(8,128)(2,1)} %param.16) | data formatting | bytes 4194304 | tf_op args[0]
  91.6 11.2 %reshape.359 = bf16[8,2,65536]{2,1,0:T(2,128)(2,1)} reshape(bf16[4096,8,32]{2,1,0:T(8,128)(2,1)} %bitcast.207) | data formatting | bytes 4194304
  102.8 6.8 all-to-all-done.5
  113.9 7.7 copy.165
  121.6 11.2 %reshape.361 = bf16[8,2,65536]{2,1,0:T(2,128)(2,1)} reshape(bf16[4096,8,32]{2,1,0:T(8,128)(2,1)} %bitcast.200) | data formatting | bytes 4194304
  134.1 7.0 all-to-all-done.3
  145.7 8.7 reshape.358
  154.4 8.3 copy.157
  162.7 8.7 reshape.364
  171.3 9.3 %copy.169 = bf16[8,8,32,512]{3,2,1,0:T(8,128)(2,1)} copy(bf16[8,8,32,512]{2,0,3,1:T(8,128)(2,1)} %bitcast.202) | data formatting | bytes 4194304 | tf_op jit(solution)/shard_map/all_to_all | solution.py:61
  185.6 6.6 gather_fusion.2
  192.2 11.6 %broadcast_select_fusion.2 = (bf16[32,256,512]{2,1,0:T(8,128)(2,1)}, bf16[32,256,512]{2,1,0:T(8,128)(2,1)}) fusion(bf16[32,256,512]{2,1,0:T(8,128)(2,1)} %gather_fusion.2, pred[32]{0:T(512)(128)(4,1)S(1)} %broadcast_compare_fusion, bf16[32,256,512]{2,1,0:T(8,128)(2,1)} %gather_fusion), kind=kLoop, calls=%fused_computation.38 | loop fusion | flops 8388608 | bytes 33554464 | tf_op jit(solution)/shard_map/jit(_take)/select_n | solution.py:88
  203.9 102.0 %all_to_all.110 = bf16[16,2,256,512]{3,2,1,0:T(8,128)(2,1)} all-to-all(bf16[16,2,256,512]{3,2,1,0:T(8,128)(2,1)} %bitcast.198), channel_id=1, replica_groups=mesh['head'=8,'ctx'=16] {'ctx'}, dimensions={0} | all-to-all | bytes 16777216 | tf_op jit(solution)/shard_map/all_to_all | solution.py:92
  315.7 8.6 reshape.360
  324.4 9.3 %copy.164 = bf16[8,32,8,512]{3,1,2,0:T(8,128)(2,1)} copy(bf16[8,32,8,512]{1,0,3,2:T(8,128)(2,1)} %bitcast.203) | data formatting | bytes 4194304 | tf_op jit(solution)/shard_map/all_to_all | solution.py:59
  337.7 8.6 reshape.362
  346.3 9.3 %copy.166 = bf16[8,32,8,512]{3,1,2,0:T(8,128)(2,1)} copy(bf16[8,32,8,512]{1,0,3,2:T(8,128)(2,1)} %bitcast.204) | data formatting | bytes 4194304 | tf_op jit(solution)/shard_map/all_to_all | solution.py:62
  359.6 6.3 gather_fusion.1
  365.9 68.3 %all-to-all-done.6 = bf16[16,2,256,512]{3,2,1,0:T(8,128)(2,1)} async-done(((bf16[16,2,256,512]{3,2,1,0:T(8,128)(2,1)}), bf16[16,2,256,512]{3,2,1,0:T(8,128)(2,1)}, u32[]{:S(2)}, u32[]{:S(2)}) %all-to-all-start.6) | async-done | bytes 8388640 | tf_op jit(solution)/shard_map/all_to_all | solution.py:93
  434.1 6.3 gather_fusion.3
  440.4 6.5 broadcast_select_fusion.4
  450.2 9.7 %reshape_reshape.16 = bf16[4,2,768,4,128]{4,3,2,1,0:T(4,128)(2,1)} reshape(bf16[8,3,256,512]{3,2,1,0:T(8,128)(2,1)} %pad_maximum_fusion.1) | data formatting | bytes 12582912 | tf_op jit(solution)/shard_map/reshape;reshape | solution.py:35
  465.3 9.9 %reshape_reshape.13 = bf16[4,2,768,4,128]{4,3,2,1,0:T(4,128)(2,1)} reshape(bf16[8,3,256,512]{3,2,1,0:T(8,128)(2,1)} %pad_maximum_fusion) | data formatting | bytes 12582912 | tf_op jit(solution)/shard_map/reshape;reshape | solution.py:35
  475.2 65.8 %while.14 = (s32[]{:T(128)}, bf16[4,2,256,4,128]{2,4,3,1,0:T(8,128)(2,1)S(1)}, f32[4,2,768,4,128]{2,4,3,1,0:T(8,128)}, f32[4,2,768,4,128]{2,4,3,1,0:T(8,128)}, b...) while((s32[]{:T(128)}, ...), condition=%wide.region_6.9_spmd, body=%wide.region_5.8_spmd.sunk | while | flops 2030043136 | bytes 52487304 | solution.py:36
  549.3 7.1 convert_element_type.41
  556.4 7.8 copy.181
  572.5 7.1 convert_element_type.43
  579.6 7.5 copy.186
  587.2 6.9 gather_fusion.4
  594.1 6.9 gather_fusion.5
  601.0 9.4 %broadcast_select_fusion = (bf16[32,256,512]{2,1,0:T(8,128)(2,1)S(1)}, bf16[32,256,512]{2,1,0:T(8,128)(2,1)}) fusion(bf16[32,256,512]{2,1,0:T(8,128)(2,1)} %gather_fusion.5, pred[32]{0:T(512)(128)(4,1)S(1)} %compare_and_fusion, bf16[32,256,512]{2,1,0:T(8,128)(2,1)} %gather_fusion.4), kind=kLoop, calls=%fused_computation.36 | loop fusion | flops 8388608 | bytes 33554464 | tf_op jit(solution)/shard_map/jit(_take)/select_n | solution.py:153
  610.3 7.6 copy.187
  618.0 6.1 all-to-all-start.9
  624.1 16.3 %copy.182 = bf16[16,2,256,512]{3,1,2,0:T(2,128)(2,1)} copy(bf16[16,2,256,512]{3,2,1,0:T(8,128)(2,1)} %bitcast.197) | data formatting | bytes 16777216 | tf_op jit(solution)/shard_map/reshape | solution.py:150
  640.4 105.4 %all-to-all-done.9 = bf16[16,2,256,512]{3,1,2,0:T(2,128)(2,1)} async-done(((bf16[16,2,256,512]{3,1,2,0:T(2,128)(2,1)}), bf16[16,2,256,512]{3,1,2,0:T(2,128)(2,1)}, u32[]{:S(2)}, u32[]{:S(2)}) %all-to-all-start.9) | async-done | bytes 8388640 | tf_op jit(solution)/shard_map/all_to_all | solution.py:158
  773.7 10.0 %copy.188 = bf16[16,2,256,512]{3,1,0,2:T(2,128)(2,1)} copy(bf16[16,2,256,512]{3,1,2,0:T(2,128)(2,1)} %all-to-all-done.9) | data formatting | bytes 16777216 | tf_op jit(solution)/shard_map/all_to_all | solution.py:158
  783.6 13.1 %reshape.277 = bf16[32,256,512]{2,0,1:T(8,128)(2,1)} reshape(bf16[16,2,256,512]{3,1,0,2:T(2,128)(2,1)} %copy.188) | data formatting | bytes 16777216 | tf_op jit(solution)/shard_map/reshape | solution.py:170
  796.8 5.8 fusion.16
  804.6 65.5 %all-to-all-done.8 = bf16[16,2,256,512]{3,1,2,0:T(2,128)(2,1)} async-done(((bf16[16,2,256,512]{3,1,2,0:T(2,128)(2,1)}), bf16[16,2,256,512]{3,1,2,0:T(2,128)(2,1)}, u32[]{:S(2)}, u32[]{:S(2)}) %all-to-all-start.8) | async-done | bytes 8388640 | tf_op jit(solution)/shard_map/all_to_all | solution.py:157
  870.1 10.0 %copy.183 = bf16[16,2,256,512]{3,1,0,2:T(2,128)(2,1)} copy(bf16[16,2,256,512]{3,1,2,0:T(2,128)(2,1)} %all-to-all-done.8) | data formatting | bytes 16777216 | tf_op jit(solution)/shard_map/all_to_all | solution.py:157
  880.1 13.1 %reshape.273 = bf16[32,256,512]{2,0,1:T(8,128)(2,1)} reshape(bf16[16,2,256,512]{3,1,0,2:T(2,128)(2,1)} %copy.183) | data formatting | bytes 16777216 | tf_op jit(solution)/shard_map/reshape | solution.py:164
  893.2 5.8 fusion.17
  (127 shorter events, 181.2 us)
Async XLA Ops:
  0.6 15.1 %copy-start.1 = (bf16[8,32,4096]{2,1,0:T(8,128)(2,1)S(1)}, bf16[8,32,4096]{2,1,0:T(8,128)(2,1)}, u32[]{:S(2)}) copy-start(bf16[8,32,4096]{2,1,0:T(8,128)(2,1)} %param.19) | copy-start | bytes 6291460
  5.5 15.6 %all-to-all-start.1 = ((s32[16,1,2]{2,1,0:T(1,128)}), s32[16,1,2]{2,1,0:T(1,128)S(1)}, u32[]{:S(2)}, u32[]{:S(2)}) async-start(s32[16,1,2]{2,1,0:T(1,128)} %bitcast.22), calls=%async_computation.1 | async-start | bytes 16384 | tf_op jit(solution)/shard_map/all_to_all | solution.py:81
  21.2 24.7 %all-to-all-start.7 = ((f32[8,1,1024]{2,1,0:T(1,128)}), f32[8,1,1024]{2,1,0:T(1,128)S(1)}, u32[]{:S(2)}, u32[]{:S(2)}) async-start(f32[8,1,1024]{2,1,0:T(1,128)} %reshape.365), calls=%async_computation.7 | async-start | bytes 65536 | tf_op jit(solution)/shard_map/all_to_all | solution.py:64
  45.9 32.1 %all-to-all-start = ((bf16[8,2,65536]{2,1,0:T(2,128)(2,1)}), bf16[8,2,65536]{2,1,0:T(2,128)(2,1)}, u32[]{:S(2)}, u32[]{:S(2)}) async-start(bf16[8,2,65536]{2,1,0:T(2,128)(2,1)} %reshape.357), calls=%async_computation | async-start | bytes 4194304 | tf_op jit(solution)/shard_map/all_to_all | solution.py:60
  78.0 31.6 %all-to-all-start.5 = ((bf16[8,2,65536]{2,1,0:T(2,128)(2,1)}), bf16[8,2,65536]{2,1,0:T(2,128)(2,1)}, u32[]{:S(2)}, u32[]{:S(2)}) async-start(bf16[8,2,65536]{2,1,0:T(2,128)(2,1)} %reshape.363), calls=%async_computation.5 | async-start | bytes 4194304 | tf_op jit(solution)/shard_map/all_to_all | solution.py:61
  109.5 31.6 %all-to-all-start.3 = ((bf16[8,2,65536]{2,1,0:T(2,128)(2,1)}), bf16[8,2,65536]{2,1,0:T(2,128)(2,1)}, u32[]{:S(2)}, u32[]{:S(2)}) async-start(bf16[8,2,65536]{2,1,0:T(2,128)(2,1)} %reshape.359), calls=%async_computation.3 | async-start | bytes 4194304 | tf_op jit(solution)/shard_map/all_to_all | solution.py:59
  134.1 20.3 %copy-start.3 = (s32[32]{0:T(128)}, s32[32]{0:T(128)S(1)}, u32[]{:S(2)}) copy-start(s32[32]{0:T(128)S(1)} %reshape.256) | copy-start | bytes 388
  141.1 62.8 %all-to-all-start.4 = ((bf16[8,2,65536]{2,1,0:T(2,128)(2,1)}), bf16[8,2,65536]{2,1,0:T(2,128)(2,1)}, u32[]{:S(2)}, u32[]{:S(2)}) async-start(bf16[8,2,65536]{2,1,0:T(2,128)(2,1)} %reshape.361), calls=%async_computation.4 | async-start | bytes 4194304 | tf_op jit(solution)/shard_map/all_to_all | solution.py:62
  305.9 5.0 copy-start.5
  305.9 128.2 %all-to-all-start.6 = ((bf16[16,2,256,512]{3,2,1,0:T(8,128)(2,1)}), bf16[16,2,256,512]{3,2,1,0:T(8,128)(2,1)}, u32[]{:S(2)}, u32[]{:S(2)}) async-start(bf16[16,2,256,512]{3,2,1,0:T(8,128)(2,1)} %bitcast.196), calls=%async_computation.6 | async-start | bytes 16777216 | tf_op jit(solution)/shard_map/all_to_all | solution.py:93
  440.4 6.5 copy-start
  465.3 9.9 %copy-start.2 = (bf16[4,2,256,4,128]{2,4,3,1,0:T(8,128)(2,1)S(1)}, bf16[4,2,256,4,128]{2,4,3,1,0:T(8,128)(2,1)}, u32[]{:S(2)}) copy-start(bf16[4,2,256,4,128]{2,4,3,1,0:T(8,128)(2,1)} %custom-call.12) | copy-start | bytes 6291460
  618.0 127.8 %all-to-all-start.9 = ((bf16[16,2,256,512]{3,1,2,0:T(2,128)(2,1)}), bf16[16,2,256,512]{3,1,2,0:T(2,128)(2,1)}, u32[]{:S(2)}, u32[]{:S(2)}) async-start(bf16[16,2,256,512]{3,1,2,0:T(2,128)(2,1)} %copy.187), calls=%async_computation.9 | async-start | bytes 16777216 | tf_op jit(solution)/shard_map/all_to_all | solution.py:158
  745.8 124.4 %all-to-all-start.8 = ((bf16[16,2,256,512]{3,1,2,0:T(2,128)(2,1)}), bf16[16,2,256,512]{3,1,2,0:T(2,128)(2,1)}, u32[]{:S(2)}, u32[]{:S(2)}) async-start(bf16[16,2,256,512]{3,1,2,0:T(2,128)(2,1)} %copy.182), calls=%async_computation.8 | async-start | bytes 16777216 | tf_op jit(solution)/shard_map/all_to_all | solution.py:157
  783.6 13.1 %copy-start.4 = (s32[32]{0:T(128)S(1)}, s32[32]{0:T(128)}, u32[]{:S(2)}) copy-start(s32[32]{0:T(128)} %copy-done.3) | copy-start | bytes 388
where the time goes:
time: 915 us; the launch traced here: 902 us
  local copies, waits for them, and re-layouts  391 us (43%)
  waiting for transfers between devices  263 us (29%)
  blocking collectives  102 us (11%)
  matrix products  51.8 us (6%)
  starting transfers between devices  46.7 us (5%)
  other arithmetic  45.7 us (5%)
    unnamed x34, local copies, waits for them, and re-layouts  142 us
    all_to_all x1, waiting for transfers between devices, body(): lax.all_to_all(back_values, 'ctx', split_axis=0, concat_axis=0, tiled=True)  105 us
    all_to_all x1, blocking collectives, body(): lax.all_to_all(send_keys, 'ctx', split_axis=0, concat_axis=0, tiled=True)  102 us
    all_to_all x1, waiting for transfers between devices, body(): lax.all_to_all(send_values, 'ctx', split_axis=0, concat_axis=0, tiled=True)  68.3 us
    all_to_all x1, waiting for transfers between devices, body(): lax.all_to_all(back_keys, 'ctx', split_axis=0, concat_axis=0, tiled=True)  65.5 us
    another operation x4, local copies, waits for them, and re-layouts, by_pairs(): array.reshape((array.shape[0] // 2, 2) + array.shape[1:])  27.5 us
  transfers between devices with their start and end apart: 9, of which 7 were waited for; matrix products, arithmetic and copies ran while one was open for 30% of the time, Pallas kernels for 0%

commit v1 on v0

v1 whole, which is shorter than its diff:
```python
import functools
import math

import jax
import jax.numpy as jnp
from jax import lax
from jax.experimental import pallas as pl
from jax.experimental.pallas import tpu as pltpu
from jax.sharding import PartitionSpec as P

MESH = pl.DeviceIdType.MESH
F32, BF16, I32 = jnp.float32, jnp.bfloat16, jnp.int32


def dot(left, right, left_dim, right_dim):
    return lax.dot_general(
        left, right, (((left_dim,), (right_dim,)), ((), ())), preferred_element_type=F32
    )


def loop(low, high, func):
    def step(index, carry):
        func(index)
        return carry

    lax.fori_loop(low, high, step, 0)


def iota(shape, dim):
    return lax.broadcasted_iota(I32, shape, dim)


def grads(query, grad, key, value, lse_row, delta_row, allowed, scale):
    scores = dot(key, query, 1, 1) * scale
    probs = jnp.where(allowed, jnp.exp(scores - lse_row), 0.0)
    dprobs = dot(value, grad, 1, 1)
    dscores = (probs * (dprobs - delta_row)).astype(BF16)
    part_value = dot(probs.astype(BF16), grad, 1, 0)
    part_key = dot(dscores, query, 1, 0) * scale
    grad_query = dot(dscores, key, 0, 0) * scale
    return grad_query, part_key, part_value


def kernel(
    nh, nc, B, R, D, S, lane_rows,
    q_ref, k_ref, v_ref, g_ref, o_ref, lse_ref, selpad_ref, sel_ref, docs_ref,
    gq_out, gk_out, gv_out,
    xq, xk, xv, xg, curq, curk, curv, curg, snd, far, gqs, gqr, curr, gqown, parts, own, run,
    stage, go, dsend, dr, dl, auxs, auxr, selall, meta, meta_s, bsel,
    xs, xr, xl, fs, fr, gs, gr, ds, dsr, as_, ar, ss, sr, os_, ls,
):
    h, c = lax.axis_index("head"), lax.axis_index("ctx")
    rows = R // nh
    scale = D ** (-0.5)
    shift = int(math.log2(B))
    lanes = 128

    selall[...] = jnp.full(selall.shape, -1, I32)
    curr[pl.ds(c, 1)] = jnp.zeros((1, R, D), BF16)

    barrier = pltpu.get_barrier_semaphore()

    def greet_head(n):
        pl.semaphore_signal(barrier, inc=1, device_id=(lax.rem(h + n, nh), c), device_id_type=MESH)

    def greet_ctx(n):
        pl.semaphore_signal(barrier, inc=1, device_id=(h, lax.rem(c + n, nc)), device_id_type=MESH)

    loop(1, nh, greet_head)
    loop(1, nc, greet_ctx)
    pl.semaphore_wait(barrier, nh + nc - 2)

    sources, places = (q_ref, g_ref, k_ref, v_ref), (xq, xg, xk, xv)

    def columns(to, s):
        return pl.ds(pl.multiple_of(to * (S * D) + s * D, D), D)

    here = pl.ds(pl.multiple_of(h * rows, rows), rows)

    def head_copy(a, s, n):
        to = lax.rem(h + n, nh)
        return pltpu.make_async_remote_copy(
            src_ref=sources[a].at[:, :, columns(to, s)],
            dst_ref=places[a].at[s, :, here, :],
            send_sem=xs.at[a, s, n],
            recv_sem=xr.at[a, s, n],
            device_id=(to, c),
            device_id_type=MESH,
        )

    def head_local(a, s):
        return pltpu.make_async_copy(
            sources[a].at[:, :, columns(h, s)], places[a].at[s, :, here, :], xl.at[a, s]
        )

    def head_start(pair, s):
        for a in pair:
            loop(1, nh, lambda n: head_copy(a, s, n).start())
            head_local(a, s).start()

    def head_wait(pair, s):
        for a in pair:
            loop(1, nh, lambda n: head_copy(a, s, n).wait_recv())
            head_local(a, s).wait()

    go_copies = [
        pltpu.make_async_copy(ref, go.at[n], ls.at[n]) for n, ref in enumerate((g_ref, o_ref))
    ]
    for copy in go_copies:
        copy.start()

    def sel_copy(n, to):
        return pltpu.make_async_remote_copy(
            src_ref=selpad_ref, dst_ref=selall.at[c], send_sem=ss.at[n], recv_sem=sr.at[n],
            device_id=(h, to), device_id_type=MESH,
        )

    def up(n):
        return lax.rem(c + n, nc)

    def down(n):
        return lax.rem(c + nc - n, nc)

    loop(1, c + 1, lambda n: sel_copy(n, down(n)).start())

    head_start((0, 1), 0)
    head_start((0, 1), 1)

    def find(owner):
        found = 0
        for b in range(B):
            found = found + jnp.where(sel_ref[b, 0] // B == owner, b, 0)
        bsel[owner] = jnp.minimum(found, B - 1)

    loop(0, c, find)

    for copy in go_copies:
        copy.wait()
    pick = (iota((8, S * D), 1) // D == iota((8, S * D), 0)).astype(BF16)

    def delta_rows(to):
        cols = pl.ds(pl.multiple_of(to * (S * D), S * D), S * D)
        prod = go[0, :, :, cols].astype(F32) * go[1, :, :, cols].astype(F32)
        prod = prod.reshape(B * rows, S * D)
        high = prod.astype(BF16)
        low = (prod - high.astype(F32)).astype(BF16)
        dsend[to] = dot(pick, high, 1, 1) + dot(pick, low, 1, 1)

    loop(0, nh, delta_rows)

    def delta_copy(n):
        to = lax.rem(h + n, nh)
        return pltpu.make_async_remote_copy(
            src_ref=dsend.at[to], dst_ref=dr.at[h], send_sem=ds.at[n], recv_sem=dsr.at[n],
            device_id=(to, c), device_id_type=MESH,
        )

    loop(1, nh, lambda n: delta_copy(n).start())
    dr[pl.ds(h, 1)] = dsend[pl.ds(h, 1)]
    loop(1, nh, lambda n: delta_copy(n).wait_recv())
    for b in range(B):
        dl[b] = jnp.concatenate(
            [dr[n][:, b * rows : (b + 1) * rows] for n in range(nh)], axis=1
        )

    def aux_copy(n, to):
        return pltpu.make_async_remote_copy(
            src_ref=auxs.at[to], dst_ref=auxr.at[c], send_sem=as_.at[n], recv_sem=ar.at[n],
            device_id=(h, to), device_id_type=MESH,
        )

    def aux_send(n):
        to = down(n)
        b = bsel[to]
        auxs[to, 0:S, :] = lse_ref[b]
        auxs[to, S : 2 * S, :] = dl[b][0:S]
        aux_copy(n, to).start()

    loop(1, c + 1, aux_send)

    def far_copy(s, n, to):
        return pltpu.make_async_remote_copy(
            src_ref=snd.at[lax.rem(s, 2), to], dst_ref=far.at[s, c],
            send_sem=fs.at[s, n], recv_sem=fr.at[s, n], device_id=(h, to), device_id_type=MESH,
        )

    def gather(s):
        head_wait((0, 1), s)

        @pl.when(s < S - 2)
        def _():
            head_start((0, 1), s + 2)

        @pl.when(s == S - 2)
        def _():
            head_start((2, 3), 0)

        @pl.when(s == S - 1)
        def _():
            loop(1, S, lambda t: head_start((2, 3), t))

        @pl.when(s >= 2)
        def _():
            loop(1, c + 1, lambda n: far_copy(s - 2, n, down(n)).wait_send())

        curq[...] = xq[s]
        curg[...] = xg[s]

        def one(n):
            to = down(n)
            b = bsel[to]
            snd[lax.rem(s, 2), to, 0] = curq[b]
            snd[lax.rem(s, 2), to, 1] = curg[b]
            far_copy(s, n, to).start()

        loop(1, c + 1, one)

    loop(0, S, gather)

    loop(1, nc - c, lambda n: sel_copy(n, up(n)).wait_recv())
    picks = selall[...]
    hit = (picks >> shift) == c
    block_sum = lambda terms: jnp.sum(jnp.where(hit, terms, 0), axis=1)
    used = block_sum(jnp.ones_like(picks))
    local = block_sum(picks & (B - 1))
    which = block_sum(iota(picks.shape, 1))
    source, lane = iota((nc, lanes), 0), iota((nc, lanes), 1)
    order = jnp.where(used > 0, local, B)
    order = jnp.where(source > c, order, B + 1)

    def across(column):
        return jnp.sum(jnp.where(lane == source, column, 0), axis=0, keepdims=True)

    def total(terms):
        return jnp.sum(terms.astype(I32), axis=1, keepdims=True)

    inside = lane < nc
    full = [order[:, e : e + 1] * (4 * nc) + 2 * source[:, :1] + e for e in range(2)]
    full_rows = [across(column) for column in full]
    ranks = [
        sum(total((row < column) & inside) for row in full_rows) for column in full
    ]
    rank_rows = [across(column) for column in ranks]
    order_rows = [across(order[:, e : e + 1]) for e in range(2)]
    spot, spot_lane = iota((2 * nc, lanes), 0), iota((2 * nc, lanes), 1)
    at = [(row == spot) & (spot_lane < nc) for row in rank_rows]
    unit_at = sum(total(jnp.where(at[e], 2 * spot_lane + e, 0)) for e in range(2))
    block_at = sum(total(jnp.where(at[e], order_rows[e], 0)) for e in range(2))
    block, block_lane = iota((8, lanes), 0), iota((8, lanes), 1)
    last = sum(total((row <= block) & (block_lane < nc)) for row in order_rows) - 1
    has = sum(total((row == block) & (block_lane < nc)) for row in order_rows)

    def table(shape_lane, items):
        out = jnp.zeros(shape_lane.shape, I32)
        for n, item in enumerate(items):
            out = jnp.where(shape_lane == n, item, out)
        return out

    meta[0 : 2 * nc] = table(spot_lane, (unit_at, block_at))
    meta[2 * nc : 3 * nc] = table(
        lane, (local[:, 0:1], local[:, 1:2], used[:, 0:1], which[:, 0:1])
    )
    meta[3 * nc : 3 * nc + 8] = table(block_lane, (jnp.maximum(last, 0), has))
    to_scalar = pltpu.make_async_copy(meta, meta_s, ls.at[0])
    to_scalar.start()
    to_scalar.wait()

    loop(1, nc - c, lambda n: aux_copy(n, up(n)).wait_recv())

    def doc_of(positions):
        end, doc = 0, jnp.zeros(positions.shape, I32)
        for n in range(docs_ref.shape[0]):
            end = end + docs_ref[n]
            doc = doc + (positions >= end).astype(I32)
        return doc

    row_lane, row_sub = iota((1, R), 1), iota((R, 1), 0)
    causal = row_sub <= row_lane

    def back_copy(s, n, to):
        return pltpu.make_async_remote_copy(
            src_ref=gqs.at[s, to], dst_ref=gqr.at[s, c], send_sem=gs.at[s, n],
            recv_sem=gr.at[s, n], device_id=(h, to), device_id_type=MESH,
        )

    def out_copy(s, n):
        ref = (gq_out, gk_out, gv_out)[n]
        return pltpu.make_async_copy(
            stage.at[s, n], ref.at[:, :, pl.ds(pl.multiple_of(s * D, D), D)], os_.at[s, n]
        )

    def finish_query(s):
        def one(n):
            back_copy(s, n, down(n)).wait_recv()
            curr[pl.ds(down(n), 1)] = gqr[s, pl.ds(down(n), 1)]

        loop(1, c + 1, one)

        def add(b):
            owner = (sel_ref[b, 0] // B) & (nc - 1)
            stage[s, 0, b] = (gqown[s, b] + curr[owner].astype(F32)).astype(BF16)

        loop(0, B, add)
        out_copy(s, 0).start()

    def heads(s):
        head_wait((2, 3), s)
        curk[...] = xk[s]
        curv[...] = xv[s]

        def own_block(b):
            docs_lane = doc_of((c * B + b) * R + row_lane)
            docs_sub = doc_of((c * B + b) * R + row_sub)
            allowed = causal & (docs_lane == docs_sub)
            grad_query, part_key, part_value = grads(
                xq[s, b], xg[s, b], xk[s, b], xv[s, b],
                lse_ref[b, pl.ds(s, 1), :], dl[b, pl.ds(s, 1), :], allowed, scale,
            )
            gqown[s, b] = grad_query
            own[0, b] = part_key
            own[1, b] = part_value

        loop(0, B, own_block)

        def far_block(n):
            d = up(n)
            far_copy(s, n, up(n)).wait_recv()
            used_here = meta_s[2 * nc + d, 2] > 0
            docs_lane = doc_of((d * B + meta_s[2 * nc + d, 3]) * R + row_lane)
            keys, values, docs_sub = [], [], []
            for e in range(2):
                j = meta_s[2 * nc + d, e] & (B - 1)
                keys.append(curk[j])
                values.append(curv[j])
                docs_sub.append(
                    jnp.where(used_here, doc_of((c * B + j) * R + row_sub), -1)
                )
            allowed = jnp.concatenate(docs_sub, axis=0) == docs_lane
            grad_query, part_key, part_value = grads(
                far[s, d, 0], far[s, d, 1],
                jnp.concatenate(keys, axis=0), jnp.concatenate(values, axis=0),
                auxr[d, pl.ds(s, 1), :], auxr[d, pl.ds(S + s, 1), :], allowed, scale,
            )
            gqs[s, d] = grad_query.astype(BF16)
            back_copy(s, n, d).start()
            for e in range(2):
                parts[0, 2 * d + e] = part_key[e * R : (e + 1) * R].astype(BF16)
                parts[1, 2 * d + e] = part_value[e * R : (e + 1) * R].astype(BF16)

        loop(1, nc - c, far_block)

        for w in range(2):
            def add_hit(m, total_so_far):
                unit, j = meta_s[m, 0] & (2 * nc - 1), meta_s[m, 1]
                before = jnp.where(m == 0, -1, meta_s[jnp.maximum(m - 1, 0), 1])
                base = jnp.where(j == before, total_so_far, own[w, j & (B - 1)])
                total_now = base + parts[w, unit].astype(F32)
                run[m] = total_now.astype(BF16)
                return total_now

            lax.fori_loop(0, 2 * (nc - 1 - c), add_hit, jnp.zeros((R, D), F32))

            def settle(j):
                reached = meta_s[3 * nc + j, 1] > 0
                stage[s, 1 + w, j] = jnp.where(
                    reached, run[meta_s[3 * nc + j, 0] & (2 * nc - 1)], own[w, j].astype(BF16)
                )

            loop(0, B, settle)
            out_copy(s, 1 + w).start()

        @pl.when(s > 0)
        def _():
            finish_query(s - 1)

    loop(0, S, heads)
    finish_query(S - 1)

    loop(1, c + 1, lambda n: sel_copy(n, down(n)).wait_send())
    loop(1, c + 1, lambda n: aux_copy(n, down(n)).wait_send())
    loop(1, nh, lambda n: delta_copy(n).wait_send())

    def drain(s):
        for a in range(4):
            loop(1, nh, lambda n: head_copy(a, s, n).wait_send())
        loop(1, nc - c, lambda n: back_copy(s, n, up(n)).wait_send())
        for n in range(3):
            out_copy(s, n).wait()

        @pl.when(s >= S - 2)
        def _():
            loop(1, c + 1, lambda n: far_copy(s, n, down(n)).wait_send())

    loop(0, S, drain)


def body(queries, keys, values, grad_out, attn_out, lse, selected, doc_lengths):
    B, rows, columns = queries.shape
    S = lse.shape[1]
    nh, nc = lax.axis_size("head"), lax.axis_size("ctx")
    D = columns // (S * nh)
    R = rows * nh
    selpad = jnp.pad(selected, ((0, 0), (0, 128 - selected.shape[1])))
    any_, vmem, smem = (
        pl.BlockSpec(memory_space=space) for space in (pl.ANY, pltpu.VMEM, pltpu.SMEM)
    )
    out = jax.ShapeDtypeStruct((B, R, S * D), BF16)
    dma = pltpu.SemaphoreType.DMA
    block = (R, D)
    scratch = [
        pltpu.VMEM((S, B) + block, BF16),
        pltpu.VMEM((S, B) + block, BF16),
        pltpu.VMEM((S, B) + block, BF16),
        pltpu.VMEM((S, B) + block, BF16),
        pltpu.VMEM((B,) + block, BF16),
        pltpu.VMEM((B,) + block, BF16),
        pltpu.VMEM((B,) + block, BF16),
        pltpu.VMEM((B,) + block, BF16),
        pltpu.VMEM((2, nc, 2) + block, BF16),
        pltpu.VMEM((S, nc, 2) + block, BF16),
        pltpu.VMEM((S, nc) + block, BF16),
        pltpu.VMEM((S, nc) + block, BF16),
        pltpu.VMEM((nc,) + block, BF16),
        pltpu.VMEM((S, B) + block, F32),
        pltpu.VMEM((2, 2 * nc) + block, BF16),
        pltpu.VMEM((2, B) + block, F32),
        pltpu.VMEM((2 * nc,) + block, BF16),
        pltpu.VMEM((S, 3, B) + block, BF16),
        pltpu.VMEM((2, B, rows, columns), BF16),
        pltpu.VMEM((nh, 8, B * rows), F32),
        pltpu.VMEM((nh, 8, B * rows), F32),
        pltpu.VMEM((B, 8, R), F32),
        pltpu.VMEM((nc, 2 * S, R), F32),
        pltpu.VMEM((nc, 2 * S, R), F32),
        pltpu.VMEM((nc, B, 128), I32),
        pltpu.VMEM((3 * nc + 8, 128), I32),
        pltpu.SMEM((3 * nc + 8, 128), I32),
        pltpu.SMEM((nc,), I32),
        dma((4, S, nh)),
        dma((4, S, nh)),
        dma((4, S)),
        dma((S, nc)),
        dma((S, nc)),
        dma((S, nc)),
        dma((S, nc)),
        dma((nh,)),
        dma((nh,)),
        dma((nc,)),
        dma((nc,)),
        dma((nc,)),
        dma((nc,)),
        dma((S, 3)),
        dma((2,)),
    ]
    return pl.pallas_call(
        functools.partial(kernel, nh, nc, B, R, D, S, 128),
        out_shape=(out, out, out),
        in_specs=[any_, any_, any_, any_, any_, vmem, vmem, smem, smem],
        out_specs=(any_, any_, any_),
        scratch_shapes=scratch,
        compiler_params=pltpu.CompilerParams(
            collective_id=0, has_side_effects=True, vmem_limit_bytes=60 * 2**20
        ),
        name="block_grads",
    )(queries, keys, values, grad_out, attn_out, lse, selpad, selected, doc_lengths)


def solution(mesh):
    rows = P("ctx", "head", None)
    in_specs = (rows, rows, rows, rows, rows, rows, P("ctx", None), P())
    out_specs = (P("ctx", None, "head"),) * 3
    return jax.shard_map(body, mesh=mesh, in_specs=in_specs, out_specs=out_specs, check_vma=False)
```

time: 915 us -> 173 us (0.19)
  the two profiles are of different devices: /device:TPU:0 before, /device:TPU:124 now
where the time goes in v1:
time: 173 us; the launch traced here: 170 us
  Pallas kernels  161 us (93%)
  local copies, waits for them, and re-layouts  8.22 us (5%)
    pallas_call x1, Pallas kernels, body(): pl.pallas_call(functools.partial(kernel, nh, nc, B, R, D, S, 128), out_sh...  161 us
    unnamed x10, local copies, waits for them, and re-layouts  7.62 us

profile of v1, /device:TPU:124, one launch (start us, length us, event | category | flops | bytes accessed | tf_op | source)
XLA Modules:
  0.0 170.0 jit_solution(4038248183273179928)
XLA Ops:
  0.6 0.8 copy.11.sel_ref
  1.4 0.0 copy-start.2
  1.4 0.6 pad.4.selpad_ref
  2.0 0.0 copy-done.2
  2.0 161.1 %block_grads.1 = (bf16[8,256,512]{2,1,0:T(8,128)(2,1)}, bf16[8,256,512]{2,1,0:T(8,128)(2,1)}, bf16[8,256,512]{2,1,0:T(8,128)(2,1)}) custom-call(bf16[8,32,4096]{2,1,0:T(8,128)(2,1)} %q_ref.1, bf16[8,32,4096]{2,1,0:T(8,128)(2,1)} %k_ref.1, bf16[8,32,4096]{2,1,0:T(8,128)(2,1)} %v_ref.1, bf16[8,32,4096]{2,1,0:T(8,128)(2,1)} %g_ref.1, ...), custom_call_target="tpu_custom_call" | custom-call | tf_op jit(solution)/shard_map/block_grads/pallas_call | solution.py:455
  163.1 0.0 copy-start.1
  163.1 3.2 %copy.16 = bf16[8,256,512]{2,1,0:T(8,128)(2,1)} copy(bf16[8,256,512]{2,1,0:T(8,128)(2,1)} %get-tuple-element.6) | data formatting | bytes 4194304
  166.3 0.0 copy-done.1
  166.3 0.0 copy-start
  166.3 1.3 copy.17
  167.6 1.0 copy-done
  168.6 1.3 copy.18
Async XLA Ops:
  1.4 0.6 copy-start.2
  163.1 3.2 %copy-start.1 = (bf16[8,256,512]{2,1,0:T(8,128)(2,1)S(1)}, bf16[8,256,512]{2,1,0:T(8,128)(2,1)}, u32[]{:S(2)}) copy-start(bf16[8,256,512]{2,1,0:T(8,128)(2,1)} %get-tuple-element.7) | copy-start | bytes 6291460
  166.3 2.3 %copy-start = (bf16[8,256,512]{2,1,0:T(8,128)(2,1)S(1)}, bf16[8,256,512]{2,1,0:T(8,128)(2,1)}, u32[]{:S(2)}) copy-start(bf16[8,256,512]{2,1,0:T(8,128)(2,1)} %get-tuple-element.8) | copy-start | bytes 6291460

commit v2 on v1

--- a/solution.py
+++ b/solution.py
@@ -43,11 +43,11 @@
 
 def kernel(
     nh, nc, B, R, D, S, lane_rows,
-    q_ref, k_ref, v_ref, g_ref, o_ref, lse_ref, selpad_ref, sel_ref, docs_ref,
+    q_ref, k_ref, v_ref, g_ref, o_ref, lse_ref, sel_ref, docs_ref,
     gq_out, gk_out, gv_out,
     xq, xk, xv, xg, curq, curk, curv, curg, snd, far, gqs, gqr, curr, gqown, parts, own, run,
-    stage, go, dsend, dr, dl, auxs, auxr, selall, meta, meta_s, bsel,
-    xs, xr, xl, fs, fr, gs, gr, ds, dsr, as_, ar, ss, sr, os_, ls,
+    go, dsend, dr, dl, auxs, auxr, selown, selall, meta, meta_s, bsel,
+    xs, xr, fs, fr, gs, gr, ds, dsr, as_, ar, ss, sr, ls,
 ):
     h, c = lax.axis_index("head"), lax.axis_index("ctx")
     rows = R // nh
@@ -56,6 +56,12 @@
     lanes = 128
 
     selall[...] = jnp.full(selall.shape, -1, I32)
+    own_row, own_lane = iota(selown.shape, 0), iota(selown.shape, 1)
+    sel_now = jnp.zeros(selown.shape, I32)
+    for b in range(B):
+        for e in range(2):
+            sel_now = jnp.where((own_row == b) & (own_lane == e), sel_ref[e, b], sel_now)
+    selown[...] = sel_now
     curr[pl.ds(c, 1)] = jnp.zeros((1, R, D), BF16)
 
     barrier = pltpu.get_barrier_semaphore()
@@ -68,71 +74,71 @@
 
     loop(1, nh, greet_head)
     loop(1, nc, greet_ctx)
-    pl.semaphore_wait(barrier, nh + nc - 2)
-
-    sources, places = (q_ref, g_ref, k_ref, v_ref), (xq, xg, xk, xv)
-
-    def columns(to, s):
-        return pl.ds(pl.multiple_of(to * (S * D) + s * D, D), D)
-
-    here = pl.ds(pl.multiple_of(h * rows, rows), rows)
-
-    def head_copy(a, s, n):
-        to = lax.rem(h + n, nh)
-        return pltpu.make_async_remote_copy(
-            src_ref=sources[a].at[:, :, columns(to, s)],
-            dst_ref=places[a].at[s, :, here, :],
-            send_sem=xs.at[a, s, n],
-            recv_sem=xr.at[a, s, n],
-            device_id=(to, c),
-            device_id_type=MESH,
-        )
-
-    def head_local(a, s):
-        return pltpu.make_async_copy(
-            sources[a].at[:, :, columns(h, s)], places[a].at[s, :, here, :], xl.at[a, s]
-        )
-
-    def head_start(pair, s):
-        for a in pair:
-            loop(1, nh, lambda n: head_copy(a, s, n).start())
-            head_local(a, s).start()
-
-    def head_wait(pair, s):
-        for a in pair:
-            loop(1, nh, lambda n: head_copy(a, s, n).wait_recv())
-            head_local(a, s).wait()
-
     go_copies = [
         pltpu.make_async_copy(ref, go.at[n], ls.at[n]) for n, ref in enumerate((g_ref, o_ref))
     ]
     for copy in go_copies:
         copy.start()
 
-    def sel_copy(n, to):
-        return pltpu.make_async_remote_copy(
-            src_ref=selpad_ref, dst_ref=selall.at[c], send_sem=ss.at[n], recv_sem=sr.at[n],
-            device_id=(h, to), device_id_type=MESH,
-        )
-
-    def up(n):
-        return lax.rem(c + n, nc)
-
-    def down(n):
-        return lax.rem(c + nc - n, nc)
-
-    loop(1, c + 1, lambda n: sel_copy(n, down(n)).start())
-
-    head_start((0, 1), 0)
-    head_start((0, 1), 1)
-
     def find(owner):
         found = 0
         for b in range(B):
-            found = found + jnp.where(sel_ref[b, 0] // B == owner, b, 0)
+            found = found + jnp.where(sel_ref[0, b] // B == owner, b, 0)
         bsel[owner] = jnp.minimum(found, B - 1)
 
-    loop(0, c, find)
+    loop(0, nc, find)
+    pl.semaphore_wait(barrier, nh + nc - 2)
+
+    def wait_bytes(ref, sem):
+        pltpu.make_async_copy(ref, ref, sem).wait()
+
+    sources, places = (q_ref, g_ref, k_ref, v_ref), (xq, xg, xk, xv)
+
+    def columns(to, s):
+        return pl.ds(pl.multiple_of(to * (S * D) + s * D, D), D)
+
+    here = pl.ds(pl.multiple_of(h * rows, rows), rows)
+
+    def head_copy(a, s, n):
+        to = h ^ n
+        return pltpu.make_async_remote_copy(
+            src_ref=sources[a].at[:, :, columns(to, s)],
+            dst_ref=places[a].at[s, :, here, :],
+            send_sem=xs.at[a],
+            recv_sem=xr.at[a, s],
+            device_id=(to, c),
+            device_id_type=MESH,
+        )
+
+    def head_local(a, s):
+        return pltpu.make_async_copy(
+            sources[a].at[:, :, columns(h, s)], places[a].at[s, :, here, :], xr.at[a, s]
+        )
+
+    def head_start(pair, s):
+        for a in pair:
+            loop(1, nh, lambda n: head_copy(a, s, n).start())
+            head_local(a, s).start()
+
+    def head_wait(pair, s):
+        for a in pair:
+            wait_bytes(places[a].at[s], xr.at[a, s])
+
+    def up(n):
+        return lax.rem(c + n, nc)
+
+    def down(n):
+        return lax.rem(c + nc - n, nc)
+
+    def sel_copy(n):
+        return pltpu.make_async_remote_copy(
+            src_ref=selown, dst_ref=selall.at[c], send_sem=ss.at[0], recv_sem=sr.at[0],
+            device_id=(h, down(n)), device_id_type=MESH,
+        )
+
+    loop(1, nc, lambda n: sel_copy(n).start())
+    head_start((0,), 0)
+    head_start((1,), 0)
 
     for copy in go_copies:
         copy.wait()
@@ -151,21 +157,63 @@
     def delta_copy(n):
         to = lax.rem(h + n, nh)
         return pltpu.make_async_remote_copy(
-            src_ref=dsend.at[to], dst_ref=dr.at[h], send_sem=ds.at[n], recv_sem=dsr.at[n],
+            src_ref=dsend.at[to], dst_ref=dr.at[h], send_sem=ds.at[0], recv_sem=dsr.at[0],
             device_id=(to, c), device_id_type=MESH,
         )
 
     loop(1, nh, lambda n: delta_copy(n).start())
     dr[pl.ds(h, 1)] = dsend[pl.ds(h, 1)]
-    loop(1, nh, lambda n: delta_copy(n).wait_recv())
+
+    def far_copy(s, n, to):
+        return pltpu.make_async_remote_copy(
+            src_ref=snd.at[s, to], dst_ref=far.at[s, c],
+            send_sem=fs.at[n], recv_sem=fr.at[s, n], device_id=(h, to), device_id_type=MESH,
+        )
+
+    def first_copy(a, n, to):
+        return pltpu.make_async_remote_copy(
+            src_ref=snd.at[0, to, a], dst_ref=far.at[0, c, a],
+            send_sem=fs.at[n], recv_sem=fr.at[0, n], device_id=(h, to), device_id_type=MESH,
+        )
+
+    def gather(s):
+        for a in range(2):
+            head_wait((a,), s)
+
+            @pl.when(s < S - 1)
+            def _():
+                head_start((a,), s + 1)
+
+            @pl.when(s == S - 1)
+            def _():
+                head_start((a + 2,), 0)
+
+        @pl.when(s == S - 1)
+        def _():
+            head_start((2, 3), 1)
+
+        curq[...] = xq[s]
+        curg[...] = xg[s]
+
+        def one(n):
+            to = down(n)
+            b = bsel[to]
+            snd[s, to, 0] = curq[b]
+            snd[s, to, 1] = curg[b]
+            far_copy(s, n, to).start()
+
+        loop(1, c + 1, one)
+
+    gather(0)
+    wait_bytes(dr.at[pl.ds(0, nh - 1)], dsr.at[0])
     for b in range(B):
         dl[b] = jnp.concatenate(
             [dr[n][:, b * rows : (b + 1) * rows] for n in range(nh)], axis=1
         )
 
-    def aux_copy(n, to):
-        return pltpu.make_async_remote_copy(
-            src_ref=auxs.at[to], dst_ref=auxr.at[c], send_sem=as_.at[n], recv_sem=ar.at[n],
+    def aux_copy(to):
+        return pltpu.make_async_remote_copy(
+            src_ref=auxs.at[to], dst_ref=auxr.at[c], send_sem=as_.at[0], recv_sem=ar.at[0],
             device_id=(h, to), device_id_type=MESH,
         )
 
@@ -174,50 +222,13 @@
         b = bsel[to]
         auxs[to, 0:S, :] = lse_ref[b]
         auxs[to, S : 2 * S, :] = dl[b][0:S]
-        aux_copy(n, to).start()
-
-    loop(1, c + 1, aux_send)
-
-    def far_copy(s, n, to):
-        return pltpu.make_async_remote_copy(
-            src_ref=snd.at[lax.rem(s, 2), to], dst_ref=far.at[s, c],
-            send_sem=fs.at[s, n], recv_sem=fr.at[s, n], device_id=(h, to), device_id_type=MESH,
-        )
-
-    def gather(s):
-        head_wait((0, 1), s)
-
-        @pl.when(s < S - 2)
-        def _():
-            head_start((0, 1), s + 2)
-
-        @pl.when(s == S - 2)
-        def _():
-            head_start((2, 3), 0)
-
-        @pl.when(s == S - 1)
-        def _():
-            loop(1, S, lambda t: head_start((2, 3), t))
-
-        @pl.when(s >= 2)
-        def _():
-            loop(1, c + 1, lambda n: far_copy(s - 2, n, down(n)).wait_send())
-
-        curq[...] = xq[s]
-        curg[...] = xg[s]
-
-        def one(n):
-            to = down(n)
-            b = bsel[to]
-            snd[lax.rem(s, 2), to, 0] = curq[b]
-            snd[lax.rem(s, 2), to, 1] = curg[b]
-            far_copy(s, n, to).start()
-
-        loop(1, c + 1, one)
-
-    loop(0, S, gather)
-
-    loop(1, nc - c, lambda n: sel_copy(n, up(n)).wait_recv())
+        aux_copy(to).start()
+
+    loop(1, nc, aux_send)
+
+    loop(1, S, gather)
+
+    wait_bytes(selall.at[pl.ds(0, nc - 1)], sr.at[0])
     picks = selall[...]
     hit = (picks >> shift) == c
     block_sum = lambda terms: jnp.sum(jnp.where(hit, terms, 0), axis=1)
@@ -265,7 +276,7 @@
     to_scalar.start()
     to_scalar.wait()
 
-    loop(1, nc - c, lambda n: aux_copy(n, up(n)).wait_recv())
+    wait_bytes(auxr.at[pl.ds(0, nc - 1)], ar.at[0])
 
     def doc_of(positions):
         end, doc = 0, jnp.zeros(positions.shape, I32)
@@ -279,32 +290,34 @@
 
     def back_copy(s, n, to):
         return pltpu.make_async_remote_copy(
-            src_ref=gqs.at[s, to], dst_ref=gqr.at[s, c], send_sem=gs.at[s, n],
-            recv_sem=gr.at[s, n], device_id=(h, to), device_id_type=MESH,
-        )
-
-    def out_copy(s, n):
-        ref = (gq_out, gk_out, gv_out)[n]
-        return pltpu.make_async_copy(
-            stage.at[s, n], ref.at[:, :, pl.ds(pl.multiple_of(s * D, D), D)], os_.at[s, n]
-        )
+            src_ref=gqs.at[s, to], dst_ref=gqr.at[s, c], send_sem=gs.at[n],
+            recv_sem=gr.at[(s + 1) // S, n], device_id=(h, to), device_id_type=MESH,
+        )
+
+    def out_cols(s):
+        return pl.ds(pl.multiple_of(s * D, D), D)
 
     def finish_query(s):
         def one(n):
-            back_copy(s, n, down(n)).wait_recv()
             curr[pl.ds(down(n), 1)] = gqr[s, pl.ds(down(n), 1)]
 
         loop(1, c + 1, one)
 
         def add(b):
-            owner = (sel_ref[b, 0] // B) & (nc - 1)
-            stage[s, 0, b] = (gqown[s, b] + curr[owner].astype(F32)).astype(BF16)
+            owner = (sel_ref[0, b] // B) & (nc - 1)
+            total = gqown[s, b] + curr[owner].astype(F32)
+            gq_out[b, :, out_cols(s)] = total.astype(BF16)
 
         loop(0, B, add)
-        out_copy(s, 0).start()
 
     def heads(s):
-        head_wait((2, 3), s)
+        for a in (2, 3):
+            head_wait((a,), s)
+
+            @pl.when(s < S - 2)
+            def _():
+                head_start((a,), s + 2)
+
         curk[...] = xk[s]
         curv[...] = xv[s]
 
@@ -362,36 +375,25 @@
 
             def settle(j):
                 reached = meta_s[3 * nc + j, 1] > 0
-                stage[s, 1 + w, j] = jnp.where(
+                (gk_out, gv_out)[w][j, :, out_cols(s)] = jnp.where(
                     reached, run[meta_s[3 * nc + j, 0] & (2 * nc - 1)], own[w, j].astype(BF16)
                 )
 
             loop(0, B, settle)
-            out_copy(s, 1 + w).start()
-
-        @pl.when(s > 0)
-        def _():
-            finish_query(s - 1)
 
     loop(0, S, heads)
+    loop(1, c + 1, lambda n: wait_bytes(gqr.at[0 : S - 1, down(n)], gr.at[0, n]))
+    loop(0, S - 1, finish_query)
+    loop(1, c + 1, lambda n: wait_bytes(gqr.at[S - 1, down(n)], gr.at[1, n]))
     finish_query(S - 1)
 
-    loop(1, c + 1, lambda n: sel_copy(n, down(n)).wait_send())
-    loop(1, c + 1, lambda n: aux_copy(n, down(n)).wait_send())
-    loop(1, nh, lambda n: delta_copy(n).wait_send())
-
-    def drain(s):
-        for a in range(4):
-            loop(1, nh, lambda n: head_copy(a, s, n).wait_send())
-        loop(1, nc - c, lambda n: back_copy(s, n, up(n)).wait_send())
-        for n in range(3):
-            out_copy(s, n).wait()
-
-        @pl.when(s >= S - 2)
-        def _():
-            loop(1, c + 1, lambda n: far_copy(s, n, down(n)).wait_send())
-
-    loop(0, S, drain)
+    wait_bytes(selall.at[pl.ds(0, nc - 1)], ss.at[0])
+    wait_bytes(auxs.at[pl.ds(0, nc - 1)], as_.at[0])
+    wait_bytes(dsend.at[pl.ds(0, nh - 1)], ds.at[0])
+    for a in range(4):
+        wait_bytes(places[a].at[:, :, pl.ds(0, R - rows), :], xs.at[a])
+    loop(1, c + 1, lambda n: wait_bytes(snd.at[:, down(n)], fs.at[n]))
+    loop(1, nc - c, lambda n: wait_bytes(gqs.at[:, up(n)], gs.at[n]))
 
 
 def body(queries, keys, values, grad_out, attn_out, lse, selected, doc_lengths):
@@ -400,11 +402,11 @@
     nh, nc = lax.axis_size("head"), lax.axis_size("ctx")
     D = columns // (S * nh)
     R = rows * nh
-    selpad = jnp.pad(selected, ((0, 0), (0, 128 - selected.shape[1])))
     any_, vmem, smem = (
         pl.BlockSpec(memory_space=space) for space in (pl.ANY, pltpu.VMEM, pltpu.SMEM)
     )
-    out = jax.ShapeDtypeStruct((B, R, S * D), BF16)
+    shape = (B, R, S * D)
+    out = pltpu.VMEM(shape, BF16)
     dma = pltpu.SemaphoreType.DMA
     block = (R, D)
     scratch = [
@@ -416,7 +418,7 @@
         pltpu.VMEM((B,) + block, BF16),
         pltpu.VMEM((B,) + block, BF16),
         pltpu.VMEM((B,) + block, BF16),
-        pltpu.VMEM((2, nc, 2) + block, BF16),
+        pltpu.VMEM((S, nc, 2) + block, BF16),
         pltpu.VMEM((S, nc, 2) + block, BF16),
         pltpu.VMEM((S, nc) + block, BF16),
         pltpu.VMEM((S, nc) + block, BF16),
@@ -425,44 +427,42 @@
         pltpu.VMEM((2, 2 * nc) + block, BF16),
         pltpu.VMEM((2, B) + block, F32),
         pltpu.VMEM((2 * nc,) + block, BF16),
-        pltpu.VMEM((S, 3, B) + block, BF16),
         pltpu.VMEM((2, B, rows, columns), BF16),
         pltpu.VMEM((nh, 8, B * rows), F32),
         pltpu.VMEM((nh, 8, B * rows), F32),
         pltpu.VMEM((B, 8, R), F32),
         pltpu.VMEM((nc, 2 * S, R), F32),
         pltpu.VMEM((nc, 2 * S, R), F32),
+        pltpu.VMEM((B, 128), I32),
         pltpu.VMEM((nc, B, 128), I32),
         pltpu.VMEM((3 * nc + 8, 128), I32),
         pltpu.SMEM((3 * nc + 8, 128), I32),
         pltpu.SMEM((nc,), I32),
-        dma((4, S, nh)),
-        dma((4, S, nh)),
+        dma((4,)),
         dma((4, S)),
+        dma((nc,)),
         dma((S, nc)),
-        dma((S, nc)),
-        dma((S, nc)),
-        dma((S, nc)),
-        dma((nh,)),
-        dma((nh,)),
         dma((nc,)),
-        dma((nc,)),
-        dma((nc,)),
-        dma((nc,)),
-        dma((S, 3)),
+        dma((2, nc)),
+        dma((1,)),
+        dma((1,)),
+        dma((1,)),
+        dma((1,)),
+        dma((1,)),
+        dma((1,)),
         dma((2,)),
     ]
     return pl.pallas_call(
         functools.partial(kernel, nh, nc, B, R, D, S, 128),
         out_shape=(out, out, out),
-        in_specs=[any_, any_, any_, any_, any_, vmem, vmem, smem, smem],
-        out_specs=(any_, any_, any_),
+        in_specs=[any_, any_, any_, any_, any_, vmem, smem, smem],
+        out_specs=(vmem, vmem, vmem),
         scratch_shapes=scratch,
         compiler_params=pltpu.CompilerParams(
-            collective_id=0, has_side_effects=True, vmem_limit_bytes=60 * 2**20
+            collective_id=0, has_side_effects=True, vmem_limit_bytes=54 * 2**20
         ),
         name="block_grads",
-    )(queries, keys, values, grad_out, attn_out, lse, selpad, selected, doc_lengths)
+    )(queries, keys, values, grad_out, attn_out, lse, selected.T, doc_lengths)
 
 
 def solution(mesh):

time: 173 us -> 147 us (0.85); the launches traced: 170 us -> 147 us
  Pallas kernels: 161 us -> 143 us
  local copies, waits for them, and re-layouts: 8.22 us -> 3.96 us
    pallas_call x1, Pallas kernels: 161 us -> 143 us  [body(): pl.pallas_call(functools.partial(kernel, nh, nc, B, R, D, S, 128), out_sh...]
    unnamed x10 -> x3, local copies, waits for them, and re-layouts: 7.62 us -> 3.96 us
where the time goes in v2:
time: 147 us
  Pallas kernels  143 us (97%)
  local copies, waits for them, and re-layouts  3.96 us (3%)
    pallas_call x1, Pallas kernels, body(): pl.pallas_call(functools.partial(kernel, nh, nc, B, R, D, S, 128), out_sh...  143 us
    unnamed x3, local copies, waits for them, and re-layouts  3.96 us

profile of v2, /device:TPU:124, one launch (start us, length us, event | category | flops | bytes accessed | tf_op | source)
XLA Modules:
  0.0 147.2 jit_solution(17292591932026952124)
XLA Ops:
  0.6 142.6 %block_grads.1 = (bf16[8,256,512]{2,1,0:T(8,128)(2,1)S(1)}, bf16[8,256,512]{2,1,0:T(8,128)(2,1)S(1)}, bf16[8,256,512]{2,1,0:T(8,128)(2,1)S(1)}) custom-call(bf16[8,32,4096]{2,1,0:T(8,128)(2,1)} %q_ref.1, bf16[8,32,4096]{2,1,0:T(8,128)(2,1)} %k_ref.1, bf16[8,32,4096]{2,1,0:T(8,128)(2,1)} %v_ref.1, bf16[8,32,4096]{2,1,0:T(8,128)(2,1)} %g_ref.1, ...), custom_call_target="tpu_custom_call" | custom-call | tf_op jit(solution)/shard_map/block_grads/pallas_call | solution.py:455
  143.2 1.3 copy.14
  144.6 1.3 copy.15
  145.9 1.3 copy.16

commit v3 on v2

--- a/solution.py
+++ b/solution.py
@@ -9,6 +9,7 @@
 from jax.sharding import PartitionSpec as P
 
 MESH = pl.DeviceIdType.MESH
+LOG2E = math.log2(math.e)
 F32, BF16, I32 = jnp.float32, jnp.bfloat16, jnp.int32
 
 
@@ -31,8 +32,8 @@
 
 
 def grads(query, grad, key, value, lse_row, delta_row, allowed, scale):
-    scores = dot(key, query, 1, 1) * scale
-    probs = jnp.where(allowed, jnp.exp(scores - lse_row), 0.0)
+    scores = dot(key, query, 1, 1) * (scale * LOG2E)
+    probs = jnp.where(allowed, jnp.exp2(scores - lse_row * LOG2E), 0.0)
     dprobs = dot(value, grad, 1, 1)
     dscores = (probs * (dprobs - delta_row)).astype(BF16)
     part_value = dot(probs.astype(BF16), grad, 1, 0)
@@ -56,37 +57,34 @@
     lanes = 128
 
     selall[...] = jnp.full(selall.shape, -1, I32)
+    curr[pl.ds(c, 1)] = jnp.zeros((1, R, D), BF16)
+
+    barrier = pltpu.get_barrier_semaphore()
+
+    def greet_head(n):
+        pl.semaphore_signal(barrier, inc=1, device_id=(lax.rem(h + n, nh), c), device_id_type=MESH)
+
+    def greet_ctx(n):
+        pl.semaphore_signal(barrier, inc=1, device_id=(h, lax.rem(c + n, nc)), device_id_type=MESH)
+
+    loop(1, nh, greet_head)
+    loop(1, nc, greet_ctx)
+    go_copies = [
+        pltpu.make_async_copy(ref, go.at[n], ls.at[n]) for n, ref in enumerate((g_ref, o_ref))
+    ]
+    def find(owner):
+        found = 0
+        for b in range(B):
+            found = found + jnp.where(sel_ref[0, b] // B == owner, b, 0)
+        bsel[owner] = jnp.minimum(found, B - 1)
+
+    loop(0, nc, find)
     own_row, own_lane = iota(selown.shape, 0), iota(selown.shape, 1)
     sel_now = jnp.zeros(selown.shape, I32)
     for b in range(B):
         for e in range(2):
             sel_now = jnp.where((own_row == b) & (own_lane == e), sel_ref[e, b], sel_now)
     selown[...] = sel_now
-    curr[pl.ds(c, 1)] = jnp.zeros((1, R, D), BF16)
-
-    barrier = pltpu.get_barrier_semaphore()
-
-    def greet_head(n):
-        pl.semaphore_signal(barrier, inc=1, device_id=(lax.rem(h + n, nh), c), device_id_type=MESH)
-
-    def greet_ctx(n):
-        pl.semaphore_signal(barrier, inc=1, device_id=(h, lax.rem(c + n, nc)), device_id_type=MESH)
-
-    loop(1, nh, greet_head)
-    loop(1, nc, greet_ctx)
-    go_copies = [
-        pltpu.make_async_copy(ref, go.at[n], ls.at[n]) for n, ref in enumerate((g_ref, o_ref))
-    ]
-    for copy in go_copies:
-        copy.start()
-
-    def find(owner):
-        found = 0
-        for b in range(B):
-            found = found + jnp.where(sel_ref[0, b] // B == owner, b, 0)
-        bsel[owner] = jnp.minimum(found, B - 1)
-
-    loop(0, nc, find)
     pl.semaphore_wait(barrier, nh + nc - 2)
 
     def wait_bytes(ref, sem):
@@ -136,9 +134,11 @@
             device_id=(h, down(n)), device_id_type=MESH,
         )
 
-    loop(1, nc, lambda n: sel_copy(n).start())
     head_start((0,), 0)
     head_start((1,), 0)
+    for copy in go_copies:
+        copy.start()
+    loop(1, nc, lambda n: sel_copy(n).start())
 
     for copy in go_copies:
         copy.wait()
@@ -200,9 +200,9 @@
             b = bsel[to]
             snd[s, to, 0] = curq[b]
             snd[s, to, 1] = curg[b]
-            far_copy(s, n, to).start()
 
         loop(1, c + 1, one)
+        loop(1, c + 1, lambda n: far_copy(s, n, down(n)).start())
 
     gather(0)
     wait_bytes(dr.at[pl.ds(0, nh - 1)], dsr.at[0])
@@ -291,7 +291,7 @@
     def back_copy(s, n, to):
         return pltpu.make_async_remote_copy(
             src_ref=gqs.at[s, to], dst_ref=gqr.at[s, c], send_sem=gs.at[n],
-            recv_sem=gr.at[(s + 1) // S, n], device_id=(h, to), device_id_type=MESH,
+            recv_sem=gr.at[jnp.maximum(s - 1, 0), n], device_id=(h, to), device_id_type=MESH,
         )
 
     def out_cols(s):
@@ -360,9 +360,17 @@
                 parts[0, 2 * d + e] = part_key[e * R : (e + 1) * R].astype(BF16)
                 parts[1, 2 * d + e] = part_value[e * R : (e + 1) * R].astype(BF16)
 
+        @pl.when(s == S - 1)
+        def _():
+            loop(1, c + 1, lambda n: wait_bytes(gqr.at[0 : S - 2, down(n)], gr.at[0, n]))
+            loop(0, S - 2, finish_query)
+
         loop(1, nc - c, far_block)
 
         for w in range(2):
+            def add_two(m, total_so_far):
+                return add_hit(2 * m + 1, add_hit(2 * m, total_so_far))
+
             def add_hit(m, total_so_far):
                 unit, j = meta_s[m, 0] & (2 * nc - 1), meta_s[m, 1]
                 before = jnp.where(m == 0, -1, meta_s[jnp.maximum(m - 1, 0), 1])
@@ -371,7 +379,7 @@
                 run[m] = total_now.astype(BF16)
                 return total_now
 
-            lax.fori_loop(0, 2 * (nc - 1 - c), add_hit, jnp.zeros((R, D), F32))
+            lax.fori_loop(0, nc - 1 - c, add_two, jnp.zeros((R, D), F32))
 
             def settle(j):
                 reached = meta_s[3 * nc + j, 1] > 0
@@ -382,10 +390,9 @@
             loop(0, B, settle)
 
     loop(0, S, heads)
-    loop(1, c + 1, lambda n: wait_bytes(gqr.at[0 : S - 1, down(n)], gr.at[0, n]))
-    loop(0, S - 1, finish_query)
-    loop(1, c + 1, lambda n: wait_bytes(gqr.at[S - 1, down(n)], gr.at[1, n]))
-    finish_query(S - 1)
+    for t in (S - 2, S - 1):
+        loop(1, c + 1, lambda n: wait_bytes(gqr.at[t, down(n)], gr.at[t - 1, n]))
+        finish_query(t)
 
     wait_bytes(selall.at[pl.ds(0, nc - 1)], ss.at[0])
     wait_bytes(auxs.at[pl.ds(0, nc - 1)], as_.at[0])
@@ -443,7 +450,7 @@
         dma((nc,)),
         dma((S, nc)),
         dma((nc,)),
-        dma((2, nc)),
+        dma((3, nc)),
         dma((1,)),
         dma((1,)),
         dma((1,)),

time: 147 us -> 147 us (level)
  no operation moved by 1% of the time
where the time goes in v3:
time: 147 us
  Pallas kernels  142 us (97%)
  local copies, waits for them, and re-layouts  3.96 us (3%)
    pallas_call x1, Pallas kernels, body(): pl.pallas_call(functools.partial(kernel, nh, nc, B, R, D, S, 128), out_sh...  142 us
    unnamed x3, local copies, waits for them, and re-layouts  3.96 us

profile of v3, /device:TPU:124, one launch (start us, length us, event | category | flops | bytes accessed | tf_op | source)
XLA Modules:
  0.0 146.6 jit_solution(17515650563884302703)
XLA Ops:
  0.6 142.0 %block_grads.1 = (bf16[8,256,512]{2,1,0:T(8,128)(2,1)S(1)}, bf16[8,256,512]{2,1,0:T(8,128)(2,1)S(1)}, bf16[8,256,512]{2,1,0:T(8,128)(2,1)S(1)}) custom-call(bf16[8,32,4096]{2,1,0:T(8,128)(2,1)} %q_ref.1, bf16[8,32,4096]{2,1,0:T(8,128)(2,1)} %k_ref.1, bf16[8,32,4096]{2,1,0:T(8,128)(2,1)} %v_ref.1, bf16[8,32,4096]{2,1,0:T(8,128)(2,1)} %g_ref.1, ...), custom_call_target="tpu_custom_call" | custom-call | tf_op jit(solution)/shard_map/block_grads/pallas_call | solution.py:462
  142.6 1.3 copy.14
  143.9 1.3 copy.15
  145.3 1.3 copy.16
